TPU v7x, 32 devices: a whole 2x2x4 slice. The times are simulated.
32 devices in a mesh: member: 2 (over y), tile: 4 (over z), face: 4 (over x, core).
Axes of the slice: x: 2, y: 2, z: 4, core: 2. Of those that a mesh axis runs over, the one named last changes fastest.
Arguments:
- atmosphere: float32 [6, 4, 16, 32, 32], P('member', 'face', None, 'tile'), parts along dimension 0, may hold values from -6 to 6
- weight_in: bfloat16 [3, 3, 90, 16], replicated, may hold values from -0.5 to 0.5
- weight_block: bfloat16 [3, 3, 90, 90], replicated, may hold values from -0.21875 to 0.21875
- weight_mix: bfloat16 [90, 90], replicated, may hold values from -0.625 to 0.625
- weight_down: bfloat16 [3, 3, 180, 90], replicated, may hold values from -0.21875 to 0.21875
- weight_coarse: bfloat16 [3, 3, 180, 180], replicated, may hold values from -0.15625 to 0.15625
- weight_decode: bfloat16 [3, 3, 90, 270], replicated, may hold values from -0.125 to 0.125
- readout_matrix: bfloat16 [16, 90], replicated, may hold values from -0.625 to 0.625
Outputs:
- advanced_state: float32 [6, 4, 16, 32, 32], P('member', 'face', None, 'tile'), parts along dimension 0
There are 2 independent parts, one for each index of `member`. A program takes and returns all parts, laid end to end along the dimension named above; an argument that names none is the same for every part. Nothing has to cross between parts.
All inputs are finite; a program needn't handle non-finite values.
Results may differ from a plain program's by a relative error of at most 0.0021.
Values may be sent and summed in bfloat16 or wider, within the bound.
A program may use at most 128 MiB of HBM per device.

v0:
```python
import jax
import jax.numpy as jnp
from jax import lax
from jax.sharding import PartitionSpec as P


def passed_along(block, axis, distance):
    devices = range(lax.axis_size(axis))
    route = [((i - distance) % len(devices), i) for i in devices]
    return lax.ppermute(block, axis, route)


def padded_2(array, sides, width):
    for axis, dim in sides:
        size, length = (lax.axis_size(axis), array.shape[dim])
        up = [(i, (i + 1) % size) for i in range(size)]
        down = [(j, i) for i, j in up]
        last = lax.slice_in_dim(array, length - width, length, axis=dim)
        initial = lax.slice_in_dim(array, 0, width, axis=dim)
        before = lax.ppermute(last, axis, up)
        after = lax.ppermute(initial, axis, down)
        array = jnp.concatenate([before, array, after], axis=dim)
    return array


def zero_corners(rim_rows, halo_width):
    corner = jnp.zeros(rim_rows.shape[:-1] + (halo_width,), rim_rows.dtype)
    return jnp.concatenate([corner, rim_rows[..., halo_width:-halo_width], corner], -1)


def turned_rows(column_block, halo_width):
    corner = jnp.zeros(column_block.shape[:-2] + (halo_width, halo_width), column_block.dtype)
    turned_strip = jnp.flip(jnp.swapaxes(column_block, -1, -2), -2)
    return jnp.concatenate([corner, turned_strip, corner], -1)


def pad_strip(strip_data, halo_width):
    row_count = strip_data.shape[2]
    col_count = strip_data.shape[3]
    tile_count = lax.axis_size("tile")
    tile_pos = lax.axis_index("tile")
    rim_start = col_count - halo_width
    polar_rows = jnp.stack(
        [strip_data[0, :, :halo_width, :], strip_data[2, :, row_count - halo_width :, :]]
    )
    west_cols = jnp.stack([strip_data[0, :, :, rim_start:], strip_data[1, :, :, rim_start:]])
    polar_prev, preceding_sunset_neighbour = passed_along((polar_rows, west_cols), "face", 1)
    east_cols = jnp.stack(
        [
            strip_data[1, :, :, :halo_width],
            strip_data[2, :, :, :halo_width],
            strip_data[0, :, :, :halo_width],
            strip_data[2, :, :, rim_start:],
        ]
    )
    following_sunrise_neighbour = passed_along(east_cols, "face", -1)
    polar_cols = lax.all_gather(following_sunrise_neighbour[2:], "tile", axis=2, tiled=True)
    owner_mask = jnp.stack([tile_pos == 0, tile_pos == tile_count - 1]).reshape(2, 1, 1, 1)
    masked_rows = jnp.where(owner_mask, polar_prev, jnp.zeros_like(polar_prev)).astype(jnp.float32)
    pieces = lax.psum_scatter(
        masked_rows.astype(jnp.bfloat16), "tile", scatter_dimension=3, tiled=True
    )
    left_cols = jnp.stack(
        [
            jnp.flip(jnp.swapaxes(pieces[0], -1, -2), -1),
            preceding_sunset_neighbour[0],
            preceding_sunset_neighbour[1],
        ]
    )
    right_cols = jnp.stack(
        [
            following_sunrise_neighbour[0],
            following_sunrise_neighbour[1],
            jnp.flip(jnp.swapaxes(pieces[1], -1, -2), -1),
        ]
    )
    extended = jnp.concatenate([left_cols, strip_data, right_cols], -1)
    padded = padded_2(extended, (("tile", 2),), halo_width)
    upper_got = padded[:, :, :halo_width, :]
    lower_got = padded[:, :, padded.shape[2] - halo_width :, :]
    upper_face = jnp.stack(
        [
            turned_rows(polar_cols[0], halo_width),
            zero_corners(upper_got[0], halo_width),
            zero_corners(upper_got[1], halo_width),
        ]
    )
    lower_face = jnp.stack(
        [
            zero_corners(lower_got[1], halo_width),
            zero_corners(lower_got[2], halo_width),
            turned_rows(polar_cols[1], halo_width),
        ]
    )
    upper_rows = jnp.where(tile_pos == 0, upper_face, upper_got)
    lower_rows = jnp.where(tile_pos == tile_count - 1, lower_face, lower_got)
    return jnp.concatenate(
        [upper_rows, padded[:, :, halo_width : padded.shape[2] - halo_width, :], lower_rows], 2
    )


def convolve(padded, weight, dilation):
    row_count = padded.shape[2] - 2 * dilation
    col_count = padded.shape[3] - 2 * dilation
    summed = None
    for row_tap in range(3):
        for col_tap in range(3):
            window_patch = padded[
                :,
                :,
                row_tap * dilation : row_tap * dilation + row_count,
                col_tap * dilation : col_tap * dilation + col_count,
            ]
            product = jnp.einsum(
                "oc,fcrn->forn",
                weight[row_tap, col_tap],
                window_patch,
                preferred_element_type=jnp.float32,
            )
            summed = product if summed is None else summed + product
    return summed


def pool_cells(values):
    shape = values.shape
    wide = values.astype(jnp.float32).reshape(shape[:-2] + (shape[-2] // 2, 2, shape[-1] // 2, 2))
    return jnp.mean(wide, axis=(-3, -1))


def upsample(values):
    shape = values.shape
    grown = jnp.broadcast_to(
        values[..., :, None, :, None], shape[:-2] + (shape[-2], 2, shape[-1], 2)
    )
    return grown.reshape(shape[:-2] + (2 * shape[-2], 2 * shape[-1]))


def per_cell_channel_blend(weight, values):
    return jnp.einsum("oc,fcrn->forn", weight, values, preferred_element_type=jnp.float32)


def shards(
    atmosphere,
    weight_in,
    weight_block,
    weight_mix,
    weight_down,
    weight_coarse,
    weight_decode,
    readout_matrix,
):
    variable_grids = atmosphere[:, 0]
    source = variable_grids.astype(jnp.bfloat16)
    encoded = jax.nn.gelu(convolve(pad_strip(source, 1), weight_in, 1)).astype(jnp.bfloat16)
    inner_out = jax.nn.gelu(convolve(pad_strip(encoded, 1), weight_block, 1)).astype(jnp.bfloat16)
    skip_level = (
        encoded.astype(jnp.float32) + per_cell_channel_blend(weight_mix, inner_out)
    ).astype(jnp.bfloat16)
    pooled = pool_cells(skip_level).astype(jnp.bfloat16)
    coarse_one = jax.nn.gelu(convolve(pad_strip(pooled, 2), weight_down, 2)).astype(jnp.bfloat16)
    coarse_two = (
        coarse_one.astype(jnp.float32)
        + jax.nn.gelu(convolve(pad_strip(coarse_one, 1), weight_coarse, 1))
    ).astype(jnp.bfloat16)
    joined_features = jnp.concatenate([upsample(coarse_two), skip_level], 1)
    padded = pad_strip(joined_features, 1)
    upscaled_activations = jax.nn.gelu(convolve(padded, weight_decode, 1)).astype(jnp.bfloat16)
    advanced_state = variable_grids + per_cell_channel_blend(readout_matrix, upscaled_activations)
    return advanced_state[:, None]


def solution(mesh):
    in_specs = (P("member", "face", None, "tile", None), P(), P(), P(), P(), P(), P(), P())
    out_specs = P("member", "face", None, "tile", None)
    return jax.shard_map(shards, mesh=mesh, in_specs=in_specs, out_specs=out_specs, check_vma=False)
```

profile of v0, /device:TPU:0, one launch (start us, length us, event | category | flops | bytes accessed | tf_op | source)
XLA Modules:
  0.0 224.8 jit_solution(17048535610313699755)
XLA Ops:
  8.3 2.7 %collective-permute-start.2 = (bf16[2,16,8,1]{3,1,2,0:T(8,128)(2,1)S(1)}, bf16[2,16,8,1]{3,1,2,0:T(8,128)(2,1)S(1)}, u32[]{:S(2)}, u32[]{:S(2)}) collective-permute-start(bf16[2,16,8,1]{3,1,2,0:T(8,128)(2,1)S(1)} %get-tuple-element.44), channel_id=1, source_target_pairs={{3,0},{0,1},{1,2},{2,3},{7,4},{4,5},{5,6},{6,7},{11,8},{8,9},{9,10... | collective-permute-start | bytes 1544 | tf_op jit(solution)/shard_map/ppermute | solution.py:10
  13.8 13.5 %all_gather.15 = bf16[2,16,32,1]{1,0,3,2:T(2,128)(2,1)S(1)} all-gather(bf16[2,16,8,1]{1,0,3,2:T(2,128)(2,1)S(1)} %copy.152), channel_id=1, replica_groups=mesh['member'=2,'tile'=4,'face'=4] {'tile'}, dimensions={2}, use_global_device_ids=true | all-gather | bytes 2560 | tf_op jit(solution)/shard_map/all_gather | solution.py:57
  27.4 18.8 %all-reduce = bf16[2,16,1,32]{1,0,2,3:T(2,128)(2,1)S(1)} all-reduce(bf16[2,16,1,32]{1,0,2,3:T(2,128)(2,1)S(1)} %broadcast_select_fusion.1), channel_id=2, replica_groups=mesh['member'=2,'tile'=4,'face'=4] {'tile'}, use_global_device_ids=true, to_apply=%region_0.1.clone | all-reduce | flops 1024 | bytes 4096
  46.9 2.0 collective-permute-start.3
  48.9 1.5 collective-permute-done.4
  50.5 1.9 collective-permute-done.3
  55.7 1.7 collective-permute-start.6
  59.9 13.1 %all_gather.16 = bf16[2,90,32,1]{1,3,2,0:T(2,128)(2,1)S(1)} all-gather(bf16[2,90,8,1]{1,3,2,0:T(2,128)(2,1)S(1)} %get-tuple-element.94), channel_id=1, replica_groups=mesh['member'=2,'tile'=4,'face'=4] {'tile'}, dimensions={2}, use_global_device_ids=true | all-gather | bytes 14400 | tf_op jit(solution)/shard_map/all_gather | solution.py:57
  73.0 4.1 %reduce-scatter.7.cloned.1.call-done = bf16[8,180]{1,0:T(8,128)(2,1)} async-done(((bf16[32,180]{1,0:T(8,128)(2,1)}), bf16[8,180]{1,0:T(8,128)(2,1)}) %reduce-scatter.7.cloned.1.call-update) | async-done | bytes 2896
  78.7 1.6 collective-permute-start.8
  80.2 1.8 collective-permute-done.9
  82.0 2.4 %collective-permute-done.8 = bf16[3,90,1,34]{1,3,2,0:T(8,128)(2,1)S(1)} collective-permute-done((bf16[3,90,1,34]{1,3,2,0:T(8,128)(2,1)S(1)}, bf16[3,90,1,34]{1,3,2,0:T(8,128)(2,1)S(1)}, u32[]{:S(2)}, u32[]{:S(2)}) %collective-permute-start.8) | collective-permute-done | bytes 18392 | tf_op jit(solution)/shard_map/ppermute | solution.py:20
  87.3 1.8 collective-permute-start.10
  90.5 13.1 %all_gather.17 = bf16[2,90,16,2]{1,3,0,2:T(2,128)(2,1)S(1)} all-gather(bf16[2,90,4,2]{1,3,0,2:T(2,128)(2,1)S(1)} %copy.163), channel_id=1, replica_groups=mesh['member'=2,'tile'=4,'face'=4] {'tile'}, dimensions={2}, use_global_device_ids=true | all-gather | bytes 14400 | tf_op jit(solution)/shard_map/all_gather | solution.py:57
  103.7 15.5 %all-reduce.1 = bf16[2,90,2,16]{1,3,2,0:T(8,128)(2,1)S(1)} all-reduce(bf16[2,90,2,16]{1,3,2,0:T(8,128)(2,1)S(1)} %broadcast_select_fusion.3), channel_id=4, replica_groups=mesh['member'=2,'tile'=4,'face'=4] {'tile'}, use_global_device_ids=true, to_apply=%region_3.4.clone | all-reduce | flops 5760 | bytes 23040
  120.4 1.2 collective-permute-start.13
  121.5 1.8 collective-permute-done.14
  123.4 2.8 %collective-permute-done.13 = bf16[3,90,2,20]{1,3,2,0:T(8,128)(2,1)S(1)} collective-permute-done((bf16[3,90,2,20]{1,3,2,0:T(8,128)(2,1)S(1)}, bf16[3,90,2,20]{1,3,2,0:T(8,128)(2,1)S(1)}, u32[]{:S(2)}, u32[]{:S(2)}) %collective-permute-start.13) | collective-permute-done | bytes 21632 | tf_op jit(solution)/shard_map/ppermute | solution.py:20
  128.2 1.6 collective-permute-start.16
  130.3 1.2 collective-permute-done.15
  131.6 13.1 %all_gather.18 = bf16[2,180,16,1]{1,3,2,0:T(2,128)(2,1)S(1)} all-gather(bf16[2,180,4,1]{1,3,2,0:T(2,128)(2,1)S(1)} %get-tuple-element.86), channel_id=1, replica_groups=mesh['member'=2,'tile'=4,'face'=4] {'tile'}, dimensions={2}, use_global_device_ids=true | all-gather | bytes 14400 | tf_op jit(solution)/shard_map/all_gather | solution.py:57
  144.8 15.5 %all-reduce.2 = bf16[2,180,1,16]{1,3,2,0:T(8,128)(2,1)S(1)} all-reduce(bf16[2,180,1,16]{1,3,2,0:T(8,128)(2,1)S(1)} %broadcast_select_fusion.2), channel_id=5, replica_groups=mesh['member'=2,'tile'=4,'face'=4] {'tile'}, use_global_device_ids=true, to_apply=%region_4.5.clone | all-reduce | flops 5760 | bytes 23040
  161.4 1.2 collective-permute-start.18
  162.6 1.8 collective-permute-done.19
  164.4 2.8 %collective-permute-done.18 = bf16[3,180,1,18]{1,3,2,0:T(8,128)(2,1)S(1)} collective-permute-done((bf16[3,180,1,18]{1,3,2,0:T(8,128)(2,1)S(1)}, bf16[3,180,1,18]{1,3,2,0:T(8,128)(2,1)S(1)}, u32[]{:S(2)}, u32[]{:S(2)}) %collective-permute-start.18) | collective-permute-done | bytes 19472 | tf_op jit(solution)/shard_map/ppermute | solution.py:20
  170.3 2.0 collective-permute-start.20
  172.5 1.3 collective-permute-done.20
  173.7 13.1 %all_gather.19 = bf16[2,270,32,1]{1,2,3,0:T(8,128)(2,1)S(1)} all-gather(bf16[2,270,8,1]{1,2,3,0:T(8,128)(2,1)S(1)} %get-tuple-element.84), channel_id=1, replica_groups=mesh['member'=2,'tile'=4,'face'=4] {'tile'}, dimensions={2}, use_global_device_ids=true | all-gather | bytes 43200 | tf_op jit(solution)/shard_map/all_gather | solution.py:57
  187.1 16.2 %all-reduce.3 = bf16[2,270,1,32]{1,3,2,0:T(8,128)(2,1)S(1)} all-reduce(bf16[2,270,1,32]{1,3,2,0:T(8,128)(2,1)S(1)} %copy.172), channel_id=6, replica_groups=mesh['member'=2,'tile'=4,'face'=4] {'tile'}, use_global_device_ids=true, to_apply=%region_5.6.clone | all-reduce | flops 17280 | bytes 69120
  204.0 1.9 collective-permute-start.24
  206.1 2.5 %collective-permute-done.24 = bf16[3,270,1,34]{1,3,2,0:T(8,128)(2,1)S(1)} collective-permute-done((bf16[3,270,1,34]{1,3,2,0:T(8,128)(2,1)S(1)}, bf16[3,270,1,34]{1,3,2,0:T(8,128)(2,1)S(1)}, u32[]{:S(2)}, u32[]{:S(2)}) %collective-permute-start.24) | collective-permute-done | bytes 55112 | tf_op jit(solution)/shard_map/ppermute | solution.py:21
  208.7 3.6 %collective-permute-done.23 = bf16[3,270,1,34]{1,3,2,0:T(8,128)(2,1)S(1)} collective-permute-done((bf16[3,270,1,34]{1,3,2,0:T(8,128)(2,1)S(1)}, bf16[3,270,1,34]{1,3,2,0:T(8,128)(2,1)S(1)}, u32[]{:S(2)}, u32[]{:S(2)}) %collective-permute-start.23) | collective-permute-done | bytes 55112 | tf_op jit(solution)/shard_map/ppermute | solution.py:20
  (248 shorter events, 29.8 us)
Async XLA Ops:
  6.5 79.7 %copy-start = (bf16[90,90]{1,0:T(8,128)(2,1)S(1)}, bf16[90,90]{1,0:T(8,128)(2,1)}, u32[]{:S(2)}) copy-start(bf16[90,90]{1,0:T(8,128)(2,1)} %param.11) | copy-start | bytes 48604
  6.5 4.6 %copy-start.1 = (f32[3,1,16,8,32]{4,3,2,1,0:T(8,128)S(1)}, f32[3,1,16,8,32]{4,3,2,1,0:T(8,128)}, u32[]{:S(2)}) copy-start(f32[3,1,16,8,32]{4,3,2,1,0:T(8,128)} %param.8) | copy-start | bytes 147460
  6.5 4.7 %copy-start.6 = (bf16[3,3,90,16]{2,3,1,0:T(8,128)(2,1)S(1)}, bf16[3,3,90,16]{2,3,1,0:T(8,128)(2,1)}, u32[]{:S(2)}) copy-start(bf16[3,3,90,16]{2,3,1,0:T(8,128)(2,1)} %param.9) | copy-start | bytes 77764
  6.5 70.6 %reduce-scatter.7.cloned.1.call-start = ((), (), s32[]{:S(2)}) async-start(), calls=%async_computation.1 | async-start | bytes 20480
  7.6 3.9 %copy-start.8 = (u32[32]{0:T(128)S(1)}, u32[32]{0:T(128)}, u32[]{:S(2)}) copy-start(u32[32]{0:T(128)} %constant.6) | copy-start | bytes 388
  7.7 19.6 %collective-permute-start.1 = (bf16[2,16,1,32]{1,0,2,3:T(2,128)(2,1)S(1)}, bf16[2,16,1,32]{1,0,2,3:T(2,128)(2,1)S(1)}, u32[]{:S(2)}, u32[]{:S(2)}) collective-permute-start(bf16[2,16,1,32]{1,0,2,3:T(2,128)(2,1)S(1)} %copy.154), channel_id=1, source_target_pairs={{3,0},{0,1},{1,2},{2,3},{7,4},{4,5},{5,6},{6,7},{11,8},{8,9},{9,10... | collective-permute-start | bytes 6152 | tf_op jit(solution)/shard_map/ppermute | solution.py:10
  8.3 38.2 %collective-permute-start.2 = (bf16[2,16,8,1]{3,1,2,0:T(8,128)(2,1)S(1)}, bf16[2,16,8,1]{3,1,2,0:T(8,128)(2,1)S(1)}, u32[]{:S(2)}, u32[]{:S(2)}) collective-permute-start(bf16[2,16,8,1]{3,1,2,0:T(8,128)(2,1)S(1)} %get-tuple-element.44), channel_id=1, source_target_pairs={{3,0},{0,1},{1,2},{2,3},{7,4},{4,5},{5,6},{6,7},{11,8},{8,9},{9,10... | collective-permute-start | bytes 1544 | tf_op jit(solution)/shard_map/ppermute | solution.py:10
  11.1 2.6 %collective-permute-start = (bf16[4,16,8,1]{3,1,2,0:T(8,128)(2,1)S(1)}, bf16[4,16,8,1]{3,1,2,0:T(8,128)(2,1)S(1)}, u32[]{:S(2)}, u32[]{:S(2)}) collective-permute-start(bf16[4,16,8,1]{3,1,2,0:T(8,128)(2,1)S(1)} %pad_maximum_fusion.14), channel_id=1, source_target_pairs={{1,0},{2,1},{3,2},{0,3},{5,4},{6,5},{7,6},{4,7},{9,8},{10,9},{11,1... | collective-permute-start | bytes 3080 | tf_op jit(solution)/shard_map/ppermute | solution.py:10
  46.6 3.7 %collective-permute-start.4 = (bf16[3,16,1,34]{3,1,2,0:T(8,128)(2,1)S(1)}, bf16[3,16,1,34]{3,1,2,0:T(8,128)(2,1)S(1)}, u32[]{:S(2)}, u32[]{:S(2)}) collective-permute-start(bf16[3,16,1,34]{3,1,2,0:T(8,128)(2,1)S(1)} %get-tuple-element.20), channel_id=1, source_target_pairs={{4,0},{8,4},{12,8},{0,12},{5,1},{9,5},{13,9},{1,13},{6,2},{10,6},{... | collective-permute-start | bytes 9800 | tf_op jit(solution)/shard_map/ppermute | solution.py:21
  46.9 5.5 %collective-permute-start.3 = (bf16[3,16,1,34]{3,1,2,0:T(8,128)(2,1)S(1)}, bf16[3,16,1,34]{3,1,2,0:T(8,128)(2,1)S(1)}, u32[]{:S(2)}, u32[]{:S(2)}) collective-permute-start(bf16[3,16,1,34]{3,1,2,0:T(8,128)(2,1)S(1)} %get-tuple-element.21), channel_id=1, source_target_pairs={{0,4},{4,8},{8,12},{12,0},{1,5},{5,9},{9,13},{13,1},{2,6},{6,10},{... | collective-permute-start | bytes 9800 | tf_op jit(solution)/shard_map/ppermute | solution.py:20
  55.1 2.5 %copy-start.5 = (bf16[3,3,90,90]{3,2,1,0:T(8,128)(2,1)S(1)}, bf16[3,3,90,90]{3,2,1,0:T(8,128)(2,1)}, u32[]{:S(2)}) copy-start(bf16[3,3,90,90]{3,2,1,0:T(8,128)(2,1)} %param.10) | copy-start | bytes 437404
  55.6 22.3 %collective-permute-start.7 = (bf16[2,90,8,1]{1,3,2,0:T(2,128)(2,1)S(1)}, bf16[2,90,8,1]{1,3,2,0:T(2,128)(2,1)S(1)}, u32[]{:S(2)}, u32[]{:S(2)}) collective-permute-start(bf16[2,90,8,1]{1,3,2,0:T(2,128)(2,1)S(1)} %get-tuple-element.26), channel_id=1, source_target_pairs={{3,0},{0,1},{1,2},{2,3},{7,4},{4,5},{5,6},{6,7},{11,8},{8,9},{9,10... | collective-permute-start | bytes 8648 | tf_op jit(solution)/shard_map/ppermute | solution.py:10
  55.7 3.2 %collective-permute-start.6 = (bf16[2,90,1,32]{1,3,2,0:T(8,128)(2,1)S(1)}, bf16[2,90,1,32]{1,3,2,0:T(8,128)(2,1)S(1)}, u32[]{:S(2)}, u32[]{:S(2)}) collective-permute-start(bf16[2,90,1,32]{1,3,2,0:T(8,128)(2,1)S(1)} %pad_maximum_fusion.99), channel_id=1, source_target_pairs={{3,0},{0,1},{1,2},{2,3},{7,4},{4,5},{5,6},{6,7},{11,8},{8,9},{9,10... | collective-permute-start | bytes 34568 | tf_op jit(solution)/shard_map/ppermute | solution.py:10
  57.5 2.4 %collective-permute-start.5 = (bf16[4,90,8,1]{1,3,2,0:T(2,128)(2,1)S(1)}, bf16[4,90,8,1]{1,3,2,0:T(2,128)(2,1)S(1)}, u32[]{:S(2)}, u32[]{:S(2)}) collective-permute-start(bf16[4,90,8,1]{1,3,2,0:T(2,128)(2,1)S(1)} %pad_maximum_fusion.98), channel_id=1, source_target_pairs={{1,0},{2,1},{3,2},{0,3},{5,4},{6,5},{7,6},{4,7},{9,8},{10,9},{11,1... | collective-permute-start | bytes 17288 | tf_op jit(solution)/shard_map/ppermute | solution.py:10
  78.1 3.9 %collective-permute-start.9 = (bf16[3,90,1,34]{1,3,2,0:T(8,128)(2,1)S(1)}, bf16[3,90,1,34]{1,3,2,0:T(8,128)(2,1)S(1)}, u32[]{:S(2)}, u32[]{:S(2)}) collective-permute-start(bf16[3,90,1,34]{1,3,2,0:T(8,128)(2,1)S(1)} %get-tuple-element.24), channel_id=1, source_target_pairs={{4,0},{8,4},{12,8},{0,12},{5,1},{9,5},{13,9},{1,13},{6,2},{10,6},{... | collective-permute-start | bytes 55088 | tf_op jit(solution)/shard_map/ppermute | solution.py:21
  78.7 5.7 %collective-permute-start.8 = (bf16[3,90,1,34]{1,3,2,0:T(8,128)(2,1)S(1)}, bf16[3,90,1,34]{1,3,2,0:T(8,128)(2,1)S(1)}, u32[]{:S(2)}, u32[]{:S(2)}) collective-permute-start(bf16[3,90,1,34]{1,3,2,0:T(8,128)(2,1)S(1)} %get-tuple-element.25), channel_id=1, source_target_pairs={{0,4},{4,8},{8,12},{12,0},{1,5},{5,9},{9,13},{13,1},{2,6},{6,10},{... | collective-permute-start | bytes 55088 | tf_op jit(solution)/shard_map/ppermute | solution.py:20
  87.2 32.1 %collective-permute-start.12 = (bf16[2,90,4,2]{1,3,2,0:T(2,128)(2,1)S(1)}, bf16[2,90,4,2]{1,3,2,0:T(2,128)(2,1)S(1)}, u32[]{:S(2)}, u32[]{:S(2)}) collective-permute-start(bf16[2,90,4,2]{1,3,2,0:T(2,128)(2,1)S(1)} %get-tuple-element.62), channel_id=1, source_target_pairs={{3,0},{0,1},{1,2},{2,3},{7,4},{4,5},{5,6},{6,7},{11,8},{8,9},{9,10... | collective-permute-start | bytes 8648 | tf_op jit(solution)/shard_map/ppermute | solution.py:10
  87.3 3.1 %collective-permute-start.10 = (bf16[4,90,4,2]{1,3,2,0:T(2,128)(2,1)S(1)}, bf16[4,90,4,2]{1,3,2,0:T(2,128)(2,1)S(1)}, u32[]{:S(2)}, u32[]{:S(2)}) collective-permute-start(bf16[4,90,4,2]{1,3,2,0:T(2,128)(2,1)S(1)} %pad_maximum_fusion.119), channel_id=1, source_target_pairs={{1,0},{2,1},{3,2},{0,3},{5,4},{6,5},{7,6},{4,7},{9,8},{10,9},{11,1... | collective-permute-start | bytes 17288 | tf_op jit(solution)/shard_map/ppermute | solution.py:10
  89.3 14.3 %collective-permute-start.11 = (bf16[2,90,2,16]{1,3,2,0:T(8,128)(2,1)S(1)}, bf16[2,90,2,16]{1,3,2,0:T(8,128)(2,1)S(1)}, u32[]{:S(2)}, u32[]{:S(2)}) collective-permute-start(bf16[2,90,2,16]{1,3,2,0:T(8,128)(2,1)S(1)} %pad_maximum_fusion.100), channel_id=1, source_target_pairs={{3,0},{0,1},{1,2},{2,3},{7,4},{4,5},{5,6},{6,7},{11,8},{8,9},{9,10... | collective-permute-start | bytes 34568 | tf_op jit(solution)/shard_map/ppermute | solution.py:10
  119.3 4.0 %collective-permute-start.14 = (bf16[3,90,2,20]{1,3,2,0:T(8,128)(2,1)S(1)}, bf16[3,90,2,20]{1,3,2,0:T(8,128)(2,1)S(1)}, u32[]{:S(2)}, u32[]{:S(2)}) collective-permute-start(bf16[3,90,2,20]{1,3,2,0:T(8,128)(2,1)S(1)} %get-tuple-element.54), channel_id=1, source_target_pairs={{4,0},{8,4},{12,8},{0,12},{5,1},{9,5},{13,9},{1,13},{6,2},{10,6},{... | collective-permute-start | bytes 64808 | tf_op jit(solution)/shard_map/ppermute | solution.py:21
  120.4 5.8 %collective-permute-start.13 = (bf16[3,90,2,20]{1,3,2,0:T(8,128)(2,1)S(1)}, bf16[3,90,2,20]{1,3,2,0:T(8,128)(2,1)S(1)}, u32[]{:S(2)}, u32[]{:S(2)}) collective-permute-start(bf16[3,90,2,20]{1,3,2,0:T(8,128)(2,1)S(1)} %get-tuple-element.55), channel_id=1, source_target_pairs={{0,4},{4,8},{8,12},{12,0},{1,5},{5,9},{9,13},{13,1},{2,6},{6,10},{... | collective-permute-start | bytes 64808 | tf_op jit(solution)/shard_map/ppermute | solution.py:20
  127.4 2.7 %copy-start.2 = (bf16[3,3,180,180]{3,2,1,0:T(8,128)(2,1)S(1)}, bf16[3,3,180,180]{3,2,1,0:T(8,128)(2,1)}, u32[]{:S(2)}) copy-start(bf16[3,3,180,180]{3,2,1,0:T(8,128)(2,1)} %param.13) | copy-start | bytes 1749604
  128.1 32.2 %collective-permute-start.17 = (bf16[2,180,4,1]{1,3,2,0:T(2,128)(2,1)S(1)}, bf16[2,180,4,1]{1,3,2,0:T(2,128)(2,1)S(1)}, u32[]{:S(2)}, u32[]{:S(2)}) collective-permute-start(bf16[2,180,4,1]{1,3,2,0:T(2,128)(2,1)S(1)} %get-tuple-element.38), channel_id=1, source_target_pairs={{3,0},{0,1},{1,2},{2,3},{7,4},{4,5},{5,6},{6,7},{11,8},{8,9},{9,10... | collective-permute-start | bytes 8648 | tf_op jit(solution)/shard_map/ppermute | solution.py:10
  128.2 16.5 %collective-permute-start.16 = (bf16[2,180,1,16]{1,3,2,0:T(8,128)(2,1)S(1)}, bf16[2,180,1,16]{1,3,2,0:T(8,128)(2,1)S(1)}, u32[]{:S(2)}, u32[]{:S(2)}) collective-permute-start(bf16[2,180,1,16]{1,3,2,0:T(8,128)(2,1)S(1)} %pad_maximum_fusion.102), channel_id=1, source_target_pairs={{3,0},{0,1},{1,2},{2,3},{7,4},{4,5},{5,6},{6,7},{11,8},{8,9},{9,10... | collective-permute-start | bytes 34568 | tf_op jit(solution)/shard_map/ppermute | solution.py:10
  129.8 1.7 collective-permute-start.15
  160.4 4.0 %collective-permute-start.19 = (bf16[3,180,1,18]{1,3,2,0:T(8,128)(2,1)S(1)}, bf16[3,180,1,18]{1,3,2,0:T(8,128)(2,1)S(1)}, u32[]{:S(2)}, u32[]{:S(2)}) collective-permute-start(bf16[3,180,1,18]{1,3,2,0:T(8,128)(2,1)S(1)} %get-tuple-element.36), channel_id=1, source_target_pairs={{4,0},{8,4},{12,8},{0,12},{5,1},{9,5},{13,9},{1,13},{6,2},{10,6},{... | collective-permute-start | bytes 58328 | tf_op jit(solution)/shard_map/ppermute | solution.py:21
  161.4 5.8 %collective-permute-start.18 = (bf16[3,180,1,18]{1,3,2,0:T(8,128)(2,1)S(1)}, bf16[3,180,1,18]{1,3,2,0:T(8,128)(2,1)S(1)}, u32[]{:S(2)}, u32[]{:S(2)}) collective-permute-start(bf16[3,180,1,18]{1,3,2,0:T(8,128)(2,1)S(1)} %get-tuple-element.37), channel_id=1, source_target_pairs={{0,4},{4,8},{8,12},{12,0},{1,5},{5,9},{9,13},{13,1},{2,6},{6,10},{... | collective-permute-start | bytes 58328 | tf_op jit(solution)/shard_map/ppermute | solution.py:20
  170.2 33.1 %collective-permute-start.22 = (bf16[2,270,8,1]{1,2,3,0:T(8,128)(2,1)S(1)}, bf16[2,270,8,1]{1,2,3,0:T(8,128)(2,1)S(1)}, u32[]{:S(2)}, u32[]{:S(2)}) collective-permute-start(bf16[2,270,8,1]{1,2,3,0:T(8,128)(2,1)S(1)} %get-tuple-element.12), channel_id=1, source_target_pairs={{3,0},{0,1},{1,2},{2,3},{7,4},{4,5},{5,6},{6,7},{11,8},{8,9},{9,10... | collective-permute-start | bytes 25928 | tf_op jit(solution)/shard_map/ppermute | solution.py:10
  170.3 3.5 %collective-permute-start.20 = (bf16[4,270,8,1]{1,2,3,0:T(8,128)(2,1)S(1)}, bf16[4,270,8,1]{1,2,3,0:T(8,128)(2,1)S(1)}, u32[]{:S(2)}, u32[]{:S(2)}) collective-permute-start(bf16[4,270,8,1]{1,2,3,0:T(8,128)(2,1)S(1)} %pad_maximum_fusion.95), channel_id=1, source_target_pairs={{1,0},{2,1},{3,2},{0,3},{5,4},{6,5},{7,6},{4,7},{9,8},{10,9},{11,1... | collective-permute-start | bytes 51848 | tf_op jit(solution)/shard_map/ppermute | solution.py:10
  172.4 14.5 %collective-permute-start.21 = (bf16[2,270,1,32]{1,2,3,0:T(2,128)(2,1)S(1)}, bf16[2,270,1,32]{1,2,3,0:T(2,128)(2,1)S(1)}, u32[]{:S(2)}, u32[]{:S(2)}) collective-permute-start(bf16[2,270,1,32]{1,2,3,0:T(2,128)(2,1)S(1)} %pad_maximum_fusion.31), channel_id=1, source_target_pairs={{3,0},{0,1},{1,2},{2,3},{7,4},{4,5},{5,6},{6,7},{11,8},{8,9},{9,10... | collective-permute-start | bytes 103688 | tf_op jit(solution)/shard_map/ppermute | solution.py:10
  204.0 4.6 %collective-permute-start.24 = (bf16[3,270,1,34]{1,3,2,0:T(8,128)(2,1)S(1)}, bf16[3,270,1,34]{1,3,2,0:T(8,128)(2,1)S(1)}, u32[]{:S(2)}, u32[]{:S(2)}) collective-permute-start(bf16[3,270,1,34]{1,3,2,0:T(8,128)(2,1)S(1)} %get-tuple-element.7), channel_id=1, source_target_pairs={{4,0},{8,4},{12,8},{0,12},{5,1},{9,5},{13,9},{1,13},{6,2},{10,6},{... | collective-permute-start | bytes 165248 | tf_op jit(solution)/shard_map/ppermute | solution.py:21
  205.9 6.3 %collective-permute-start.23 = (bf16[3,270,1,34]{1,3,2,0:T(8,128)(2,1)S(1)}, bf16[3,270,1,34]{1,3,2,0:T(8,128)(2,1)S(1)}, u32[]{:S(2)}, u32[]{:S(2)}) collective-permute-start(bf16[3,270,1,34]{1,3,2,0:T(8,128)(2,1)S(1)} %get-tuple-element.8), channel_id=1, source_target_pairs={{0,4},{4,8},{8,12},{12,0},{1,5},{5,9},{9,13},{13,1},{2,6},{6,10},{... | collective-permute-start | bytes 165248 | tf_op jit(solution)/shard_map/ppermute | solution.py:20
  (3 other events, 4.2 us)
Sparse Core Ops, SparseCore 0:
  60.0 17.1 reduce-scatter.6
where the time goes:
time: 225 us
  blocking collectives  132 us (59%)
  waiting for transfers between devices  32 us (14%)
  starting transfers between devices  21.5 us (10%)
  between operations  15.9 us (7%)
  matrix products  11.8 us (5%)
  local copies, waits for them, and re-layouts  7.52 us (3%)
  other arithmetic  3.83 us (2%)
    all_gather x5, blocking collectives, pad_strip(): lax.all_gather(following_sunrise_neighbour[2:], 'tile', axis=2, tiled=True)  66.1 us
    unnamed x4, blocking collectives  66 us
    ppermute x5, waiting for transfers between devices, padded_2(): before = lax.ppermute(last, axis, up)  13.5 us
    ppermute x15, starting transfers between devices, passed_along(): return lax.ppermute(block, axis, route)  11 us
    dot_general x43, matrix products, convolve(): jnp.einsum('oc,fcrn->forn', weight[row_tap, col_tap], window_patch, prefe...  10.8 us
    ppermute x5, waiting for transfers between devices, padded_2(): after = lax.ppermute(initial, axis, down)  9.37 us
    ppermute x5, starting transfers between devices, padded_2(): before = lax.ppermute(last, axis, up)  6.09 us
    ppermute x15, waiting for transfers between devices, passed_along(): return lax.ppermute(block, axis, route)  5.03 us
  transfers between devices with their start and end apart: 26, of which 16 were waited for; matrix products, arithmetic and copies ran while one was open for 2% of the time, Pallas kernels for 0%

commit v1 on v0

--- a/solution.py
+++ b/solution.py
@@ -2,6 +2,12 @@
 import jax.numpy as jnp
 from jax import lax
 from jax.sharding import PartitionSpec as P
+
+
+def joined_along(blocks, dim):
+    blocks = jnp.moveaxis(blocks, 0, dim)
+    shape = blocks.shape
+    return blocks.reshape(*shape[:dim], shape[dim] * shape[dim + 1], *shape[dim + 2 :])
 
 
 def passed_along(block, axis, distance):
@@ -54,7 +60,20 @@
         ]
     )
     following_sunrise_neighbour = passed_along(east_cols, "face", -1)
-    polar_cols = lax.all_gather(following_sunrise_neighbour[2:], "tile", axis=2, tiled=True)
+    shard = following_sunrise_neighbour[2:]
+    count = lax.axis_size("tile")
+    pairs = [(i_2, (i_2 + 1) % count) for i_2 in range(count)]
+    back = [(b, a) for a, b in pairs]
+    lower, upper = ([], [])
+    for step in range(count - 1):
+        if step % 2 == 0:
+            lower.append(lax.ppermute(lower[-1] if lower else shard, "tile", pairs))
+        else:
+            upper.append(lax.ppermute(upper[-1] if upper else shard, "tile", back))
+    tiles = jnp.stack([*lower[::-1], shard, *upper])
+    shift = lax.axis_index("tile") - len(lower)
+    tiles = tiles[(jnp.arange(count) - shift) % count]
+    polar_cols = joined_along(tiles, 2)
     owner_mask = jnp.stack([tile_pos == 0, tile_pos == tile_count - 1]).reshape(2, 1, 1, 1)
     masked_rows = jnp.where(owner_mask, polar_prev, jnp.zeros_like(polar_prev)).astype(jnp.float32)
     pieces = lax.psum_scatter(

time: 225 us -> 204 us (0.907)
  blocking collectives: 132 us -> 77.6 us
  starting transfers between devices: 21.5 us -> 49.8 us
  local copies, waits for them, and re-layouts: 7.52 us -> 10.2 us
  waiting for transfers between devices: 32 us -> 34.5 us
    all_gather x5 -> x0, blocking collectives: 66.1 us -> none  [pad_strip(): lax.all_gather(following_sunrise_neighbour[2:], 'tile', axis=2, tiled=True)]
    ppermute x0 -> x15, starting transfers between devices: none -> 20.4 us  [the longest x5 17.8 us: pad_strip(): upper.append(lax.ppermute(upper[-1] if upper else shard, 'tile', back))]
    ppermute x5, starting transfers between devices: 4.46 us -> 19.3 us  [padded_2(): after = lax.ppermute(initial, axis, down)]
    unnamed x4, blocking collectives: 66 us -> 77.6 us
    unnamed x2, waiting for transfers between devices: 4.16 us -> 15.2 us
    ppermute x0 -> x15, waiting for transfers between devices: none -> 9.98 us  [the longest x10 9.97 us: pad_strip(): lower.append(lax.ppermute(lower[-1] if lower else shard, 'tile', pairs))]
    ppermute x5, waiting for transfers between devices: 9.37 us -> 0.01 us  [padded_2(): after = lax.ppermute(initial, axis, down)]
    ppermute x5, starting transfers between devices: 6.09 us -> 0.29 us  [padded_2(): before = lax.ppermute(last, axis, up)]
  transfers between devices with their start and end apart: 26 -> 41, of which waited for: 16 -> 14; matrix products, arithmetic and copies ran while one was open for 2% -> 4% of each run, Pallas kernels for 0% -> 0%
where the time goes in v1:
time: 204 us
  blocking collectives  77.6 us (38%)
  starting transfers between devices  49.8 us (24%)
  waiting for transfers between devices  34.5 us (17%)
  between operations  16.2 us (8%)
  matrix products  12.1 us (6%)
  local copies, waits for them, and re-layouts  10.2 us (5%)
  other arithmetic  3.36 us (2%)
    unnamed x4, blocking collectives  77.6 us
    ppermute x5, starting transfers between devices, padded_2(): after = lax.ppermute(initial, axis, down)  19.3 us
    ppermute x5, starting transfers between devices, pad_strip(): upper.append(lax.ppermute(upper[-1] if upper else shard, 'tile', back))  17.8 us
    unnamed x2, waiting for transfers between devices  15.2 us
    dot_general x43, matrix products, convolve(): jnp.einsum('oc,fcrn->forn', weight[row_tap, col_tap], window_patch, prefe...  11.1 us
    ppermute x10, waiting for transfers between devices, pad_strip(): lower.append(lax.ppermute(lower[-1] if lower else shard, 'tile', pairs))  9.97 us
    ppermute x15, starting transfers between devices, passed_along(): return lax.ppermute(block, axis, route)  9.7 us
    ppermute x5, waiting for transfers between devices, padded_2(): before = lax.ppermute(last, axis, up)  8.76 us
  transfers between devices with their start and end apart: 41, of which 14 were waited for; matrix products, arithmetic and copies ran while one was open for 4% of the time, Pallas kernels for 0%

profile of v1, /device:TPU:0, one launch (start us, length us, event | category | flops | bytes accessed | tf_op | source)
XLA Modules:
  0.0 203.8 jit_solution(657361132397326893)
XLA Ops:
  6.6 1.1 copy.374
  8.8 2.0 collective-permute-start
  12.2 2.4 %collective-permute-start.1 = (bf16[2,16,8,1]{1,2,3,0:T(8,128)(2,1)S(1)}, bf16[2,16,8,1]{1,2,3,0:T(8,128)(2,1)S(1)}, u32[]{:S(2)}, u32[]{:S(2)}) collective-permute-start(bf16[2,16,8,1]{1,2,3,0:T(8,128)(2,1)S(1)} %get-tuple-element.100), channel_id=1, source_target_pairs={{0,4},{4,8},{8,12},{12,0},{1,5},{5,9},{9,13},{13,1},{2,6},{6,10},{... | collective-permute-start | bytes 1544 | tf_op jit(solution)/shard_map/ppermute | solution.py:70
  16.4 2.1 %collective-permute-start.3 = (bf16[2,16,8,1]{1,2,3,0:T(8,128)(2,1)S(1)}, bf16[2,16,8,1]{1,2,3,0:T(8,128)(2,1)S(1)}, u32[]{:S(2)}, u32[]{:S(2)}) collective-permute-start(bf16[2,16,8,1]{1,2,3,0:T(8,128)(2,1)S(1)} %get-tuple-element.100), channel_id=1, source_target_pairs={{4,0},{8,4},{12,8},{0,12},{5,1},{9,5},{13,9},{1,13},{6,2},{10,6},{... | collective-permute-start | bytes 1544 | tf_op jit(solution)/shard_map/ppermute | solution.py:72
  18.7 19.2 %all-reduce = bf16[2,16,1,32]{1,0,2,3:T(2,128)(2,1)S(1)} all-reduce(bf16[2,16,1,32]{1,0,2,3:T(2,128)(2,1)S(1)} %copy.161), channel_id=2, replica_groups=mesh['member'=2,'tile'=4,'face'=4] {'tile'}, use_global_device_ids=true, to_apply=%region_0.1.clone | all-reduce | flops 1024 | bytes 4096
  38.5 3.8 %collective-permute-start.7 = (bf16[3,16,1,34]{3,1,2,0:T(8,128)(2,1)S(1)}, bf16[3,16,1,34]{3,1,2,0:T(8,128)(2,1)S(1)}, u32[]{:S(2)}, u32[]{:S(2)}) collective-permute-start(bf16[3,16,1,34]{3,1,2,0:T(8,128)(2,1)S(1)} %get-tuple-element.11), channel_id=1, source_target_pairs={{4,0},{8,4},{12,8},{0,12},{5,1},{9,5},{13,9},{1,13},{6,2},{10,6},{... | collective-permute-start | bytes 9800 | tf_op jit(solution)/shard_map/ppermute | solution.py:27
  43.1 0.9 collective-permute-done.6
  48.1 1.4 collective-permute-start.13
  49.5 3.8 %collective-permute-start.11 = (bf16[2,90,8,1]{1,3,2,0:T(2,128)(2,1)S(1)}, bf16[2,90,8,1]{1,3,2,0:T(2,128)(2,1)S(1)}, u32[]{:S(2)}, u32[]{:S(2)}) collective-permute-start(bf16[2,90,8,1]{1,3,2,0:T(2,128)(2,1)S(1)} %get-tuple-element.83), channel_id=1, source_target_pairs={{4,0},{8,4},{12,8},{0,12},{5,1},{9,5},{13,9},{1,13},{6,2},{10,6},{... | collective-permute-start | bytes 8648 | tf_op jit(solution)/shard_map/ppermute | solution.py:72
  53.6 1.4 collective-permute-done.9
  55.9 4.5 %collective-permute-done.10 = bf16[2,90,8,1]{1,3,2,0:T(2,128)(2,1)S(1)} collective-permute-done((bf16[2,90,8,1]{1,3,2,0:T(2,128)(2,1)S(1)}, bf16[2,90,8,1]{1,3,2,0:T(2,128)(2,1)S(1)}, u32[]{:S(2)}, u32[]{:S(2)}) %collective-permute-start.10) | collective-permute-done | bytes 2912 | tf_op jit(solution)/shard_map/ppermute | solution.py:70
  61.0 15.1 %reduce-scatter.7.cloned.1.call-done = bf16[8,180]{1,0:T(8,128)(2,1)} async-done(((bf16[32,180]{1,0:T(8,128)(2,1)}), bf16[8,180]{1,0:T(8,128)(2,1)}) %reduce-scatter.7.cloned.1.call-update) | async-done | bytes 2896
  77.1 3.8 %collective-permute-start.15 = (bf16[3,90,1,34]{1,3,2,0:T(8,128)(2,1)S(1)}, bf16[3,90,1,34]{1,3,2,0:T(8,128)(2,1)S(1)}, u32[]{:S(2)}, u32[]{:S(2)}) collective-permute-start(bf16[3,90,1,34]{1,3,2,0:T(8,128)(2,1)S(1)} %get-tuple-element.15), channel_id=1, source_target_pairs={{4,0},{8,4},{12,8},{0,12},{5,1},{9,5},{13,9},{1,13},{6,2},{10,6},{... | collective-permute-start | bytes 55088 | tf_op jit(solution)/shard_map/ppermute | solution.py:27
  80.9 1.9 collective-permute-done.14
  86.2 1.1 collective-permute-start.21
  87.6 3.9 %collective-permute-start.19 = (bf16[2,90,4,2]{1,3,2,0:T(2,128)(2,1)S(1)}, bf16[2,90,4,2]{1,3,2,0:T(2,128)(2,1)S(1)}, u32[]{:S(2)}, u32[]{:S(2)}) collective-permute-start(bf16[2,90,4,2]{1,3,2,0:T(2,128)(2,1)S(1)} %get-tuple-element.95), channel_id=1, source_target_pairs={{4,0},{8,4},{12,8},{0,12},{5,1},{9,5},{13,9},{1,13},{6,2},{10,6},{... | collective-permute-start | bytes 8648 | tf_op jit(solution)/shard_map/ppermute | solution.py:72
  91.4 1.3 collective-permute-done.17
  92.9 19.2 %all-reduce.1 = bf16[2,90,2,16]{1,2,3,0:T(2,128)(2,1)S(1)} all-reduce(bf16[2,90,2,16]{1,2,3,0:T(2,128)(2,1)S(1)} %copy.172), channel_id=4, replica_groups=mesh['member'=2,'tile'=4,'face'=4] {'tile'}, use_global_device_ids=true, to_apply=%region_3.4.clone | all-reduce | flops 5760 | bytes 23040
  113.0 3.9 %collective-permute-start.23 = (bf16[3,90,2,20]{1,3,2,0:T(8,128)(2,1)S(1)}, bf16[3,90,2,20]{1,3,2,0:T(8,128)(2,1)S(1)}, u32[]{:S(2)}, u32[]{:S(2)}) collective-permute-start(bf16[3,90,2,20]{1,3,2,0:T(8,128)(2,1)S(1)} %get-tuple-element.43), channel_id=1, source_target_pairs={{4,0},{8,4},{12,8},{0,12},{5,1},{9,5},{13,9},{1,13},{6,2},{10,6},{... | collective-permute-start | bytes 64808 | tf_op jit(solution)/shard_map/ppermute | solution.py:27
  116.9 1.8 collective-permute-done.22
  121.3 0.8 collective-permute-start.29
  122.3 3.9 %collective-permute-start.27 = (bf16[2,180,4,1]{1,3,2,0:T(2,128)(2,1)S(1)}, bf16[2,180,4,1]{1,3,2,0:T(2,128)(2,1)S(1)}, u32[]{:S(2)}, u32[]{:S(2)}) collective-permute-start(bf16[2,180,4,1]{1,3,2,0:T(2,128)(2,1)S(1)} %get-tuple-element.73), channel_id=1, source_target_pairs={{4,0},{8,4},{12,8},{0,12},{5,1},{9,5},{13,9},{1,13},{6,2},{10,6},{... | collective-permute-start | bytes 8648 | tf_op jit(solution)/shard_map/ppermute | solution.py:72
  126.5 1.4 collective-permute-done.25
  128.0 19.3 %all-reduce.2 = bf16[2,180,1,16]{1,3,2,0:T(8,128)(2,1)S(1)} all-reduce(bf16[2,180,1,16]{1,3,2,0:T(8,128)(2,1)S(1)} %broadcast_select_fusion.1), channel_id=5, replica_groups=mesh['member'=2,'tile'=4,'face'=4] {'tile'}, use_global_device_ids=true, to_apply=%region_4.5.clone | all-reduce | flops 5760 | bytes 23040
  148.1 4.0 %collective-permute-start.31 = (bf16[3,180,1,18]{1,3,2,0:T(8,128)(2,1)S(1)}, bf16[3,180,1,18]{1,3,2,0:T(8,128)(2,1)S(1)}, u32[]{:S(2)}, u32[]{:S(2)}) collective-permute-start(bf16[3,180,1,18]{1,3,2,0:T(8,128)(2,1)S(1)} %get-tuple-element.25), channel_id=1, source_target_pairs={{4,0},{8,4},{12,8},{0,12},{5,1},{9,5},{13,9},{1,13},{6,2},{10,6},{... | collective-permute-start | bytes 58328 | tf_op jit(solution)/shard_map/ppermute | solution.py:27
  152.1 1.7 collective-permute-done.30
  157.4 0.8 collective-permute-start.36
  158.6 4.1 %collective-permute-start.35 = (bf16[2,270,8,1]{1,3,2,0:T(2,128)(2,1)S(1)}, bf16[2,270,8,1]{1,3,2,0:T(2,128)(2,1)S(1)}, u32[]{:S(2)}, u32[]{:S(2)}) collective-permute-start(bf16[2,270,8,1]{1,3,2,0:T(2,128)(2,1)S(1)} %get-tuple-element.49), channel_id=1, source_target_pairs={{4,0},{8,4},{12,8},{0,12},{5,1},{9,5},{13,9},{1,13},{6,2},{10,6},{... | collective-permute-start | bytes 25928 | tf_op jit(solution)/shard_map/ppermute | solution.py:72
  163.1 1.3 collective-permute-done.33
  164.6 19.9 %all-reduce.3 = bf16[2,270,1,32]{1,3,2,0:T(8,128)(2,1)S(1)} all-reduce(bf16[2,270,1,32]{1,3,2,0:T(8,128)(2,1)S(1)} %broadcast_select_fusion), channel_id=6, replica_groups=mesh['member'=2,'tile'=4,'face'=4] {'tile'}, use_global_device_ids=true, to_apply=%region_5.6.clone | all-reduce | flops 17280 | bytes 69120
  185.4 3.8 %collective-permute-start.39 = (bf16[3,270,1,34]{1,3,2,0:T(8,128)(2,1)S(1)}, bf16[3,270,1,34]{1,3,2,0:T(8,128)(2,1)S(1)}, u32[]{:S(2)}, u32[]{:S(2)}) collective-permute-start(bf16[3,270,1,34]{1,3,2,0:T(8,128)(2,1)S(1)} %get-tuple-element.7), channel_id=1, source_target_pairs={{4,0},{8,4},{12,8},{0,12},{5,1},{9,5},{13,9},{1,13},{6,2},{10,6},{... | collective-permute-start | bytes 165248 | tf_op jit(solution)/shard_map/ppermute | solution.py:27
  189.2 2.5 %collective-permute-done.38 = bf16[3,270,1,34]{1,3,2,0:T(8,128)(2,1)S(1)} collective-permute-done((bf16[3,270,1,34]{1,3,2,0:T(8,128)(2,1)S(1)}, bf16[3,270,1,34]{1,3,2,0:T(8,128)(2,1)S(1)}, u32[]{:S(2)}, u32[]{:S(2)}) %collective-permute-start.38) | collective-permute-done | bytes 55112 | tf_op jit(solution)/shard_map/ppermute | solution.py:26
  (288 shorter events, 29.4 us)
Async XLA Ops:
  6.5 69.6 %reduce-scatter.7.cloned.1.call-start = ((), (), s32[]{:S(2)}) async-start(), calls=%async_computation.1 | async-start | bytes 20480
  7.7 10.9 %collective-permute-start.4 = (bf16[2,16,1,32]{3,1,2,0:T(8,128)(2,1)S(1)}, bf16[2,16,1,32]{3,1,2,0:T(8,128)(2,1)S(1)}, u32[]{:S(2)}, u32[]{:S(2)}) collective-permute-start(bf16[2,16,1,32]{3,1,2,0:T(8,128)(2,1)S(1)} %pad_maximum_fusion.118), channel_id=1, source_target_pairs={{3,0},{0,1},{1,2},{2,3},{7,4},{4,5},{5,6},{6,7},{11,8},{8,9},{9,10... | collective-permute-start | bytes 6152 | tf_op jit(solution)/shard_map/ppermute | solution.py:16
  10.8 27.6 %collective-permute-start.5 = (bf16[2,16,8,1]{3,1,2,0:T(8,128)(2,1)S(1)}, bf16[2,16,8,1]{3,1,2,0:T(8,128)(2,1)S(1)}, u32[]{:S(2)}, u32[]{:S(2)}) collective-permute-start(bf16[2,16,8,1]{3,1,2,0:T(8,128)(2,1)S(1)} %get-tuple-element.33), channel_id=1, source_target_pairs={{3,0},{0,1},{1,2},{2,3},{7,4},{4,5},{5,6},{6,7},{11,8},{8,9},{9,10... | collective-permute-start | bytes 1544 | tf_op jit(solution)/shard_map/ppermute | solution.py:16
  12.2 6.4 %collective-permute-start.1 = (bf16[2,16,8,1]{1,2,3,0:T(8,128)(2,1)S(1)}, bf16[2,16,8,1]{1,2,3,0:T(8,128)(2,1)S(1)}, u32[]{:S(2)}, u32[]{:S(2)}) collective-permute-start(bf16[2,16,8,1]{1,2,3,0:T(8,128)(2,1)S(1)} %get-tuple-element.100), channel_id=1, source_target_pairs={{0,4},{4,8},{8,12},{12,0},{1,5},{5,9},{9,13},{13,1},{2,6},{6,10},{... | collective-permute-start | bytes 1544 | tf_op jit(solution)/shard_map/ppermute | solution.py:70
  16.4 25.9 %collective-permute-start.3 = (bf16[2,16,8,1]{1,2,3,0:T(8,128)(2,1)S(1)}, bf16[2,16,8,1]{1,2,3,0:T(8,128)(2,1)S(1)}, u32[]{:S(2)}, u32[]{:S(2)}) collective-permute-start(bf16[2,16,8,1]{1,2,3,0:T(8,128)(2,1)S(1)} %get-tuple-element.100), channel_id=1, source_target_pairs={{4,0},{8,4},{12,8},{0,12},{5,1},{9,5},{13,9},{1,13},{6,2},{10,6},{... | collective-permute-start | bytes 1544 | tf_op jit(solution)/shard_map/ppermute | solution.py:72
  18.5 23.8 %collective-permute-start.2 = (bf16[2,16,8,1]{1,2,3,0:T(8,128)(2,1)S(1)}, bf16[2,16,8,1]{1,2,3,0:T(8,128)(2,1)S(1)}, u32[]{:S(2)}, u32[]{:S(2)}) collective-permute-start(bf16[2,16,8,1]{1,2,3,0:T(8,128)(2,1)S(1)} %collective-permute-done.1), channel_id=1, source_target_pairs={{0,4},{4,8},{8,12},{12,0},{1,5},{5,9},{9,13},{13,1},{2,6},{6,10},{... | collective-permute-start | bytes 1544 | tf_op jit(solution)/shard_map/ppermute | solution.py:70
  38.4 5.5 %collective-permute-start.6 = (bf16[3,16,1,34]{3,1,2,0:T(8,128)(2,1)S(1)}, bf16[3,16,1,34]{3,1,2,0:T(8,128)(2,1)S(1)}, u32[]{:S(2)}, u32[]{:S(2)}) collective-permute-start(bf16[3,16,1,34]{3,1,2,0:T(8,128)(2,1)S(1)} %get-tuple-element.12), channel_id=1, source_target_pairs={{0,4},{4,8},{8,12},{12,0},{1,5},{5,9},{9,13},{13,1},{2,6},{6,10},{... | collective-permute-start | bytes 9800 | tf_op jit(solution)/shard_map/ppermute | solution.py:26
  38.5 5.6 %collective-permute-start.7 = (bf16[3,16,1,34]{3,1,2,0:T(8,128)(2,1)S(1)}, bf16[3,16,1,34]{3,1,2,0:T(8,128)(2,1)S(1)}, u32[]{:S(2)}, u32[]{:S(2)}) collective-permute-start(bf16[3,16,1,34]{3,1,2,0:T(8,128)(2,1)S(1)} %get-tuple-element.11), channel_id=1, source_target_pairs={{4,0},{8,4},{12,8},{0,12},{5,1},{9,5},{13,9},{1,13},{6,2},{10,6},{... | collective-permute-start | bytes 9800 | tf_op jit(solution)/shard_map/ppermute | solution.py:27
  47.5 7.5 %collective-permute-start.12 = (bf16[2,90,1,32]{1,3,2,0:T(8,128)(2,1)S(1)}, bf16[2,90,1,32]{1,3,2,0:T(8,128)(2,1)S(1)}, u32[]{:S(2)}, u32[]{:S(2)}) collective-permute-start(bf16[2,90,1,32]{1,3,2,0:T(8,128)(2,1)S(1)} %pad_maximum_fusion.96), channel_id=1, source_target_pairs={{3,0},{0,1},{1,2},{2,3},{7,4},{4,5},{5,6},{6,7},{11,8},{8,9},{9,10... | collective-permute-start | bytes 34568 | tf_op jit(solution)/shard_map/ppermute | solution.py:16
  48.1 28.9 %collective-permute-start.13 = (bf16[2,90,8,1]{1,3,2,0:T(2,128)(2,1)S(1)}, bf16[2,90,8,1]{1,3,2,0:T(2,128)(2,1)S(1)}, u32[]{:S(2)}, u32[]{:S(2)}) collective-permute-start(bf16[2,90,8,1]{1,3,2,0:T(2,128)(2,1)S(1)} %get-tuple-element.17), channel_id=1, source_target_pairs={{3,0},{0,1},{1,2},{2,3},{7,4},{4,5},{5,6},{6,7},{11,8},{8,9},{9,10... | collective-permute-start | bytes 8648 | tf_op jit(solution)/shard_map/ppermute | solution.py:16
  77.0 5.7 %collective-permute-start.14 = (bf16[3,90,1,34]{1,3,2,0:T(8,128)(2,1)S(1)}, bf16[3,90,1,34]{1,3,2,0:T(8,128)(2,1)S(1)}, u32[]{:S(2)}, u32[]{:S(2)}) collective-permute-start(bf16[3,90,1,34]{1,3,2,0:T(8,128)(2,1)S(1)} %get-tuple-element.16), channel_id=1, source_target_pairs={{0,4},{4,8},{8,12},{12,0},{1,5},{5,9},{9,13},{13,1},{2,6},{6,10},{... | collective-permute-start | bytes 55088 | tf_op jit(solution)/shard_map/ppermute | solution.py:26
  77.1 5.7 %collective-permute-start.15 = (bf16[3,90,1,34]{1,3,2,0:T(8,128)(2,1)S(1)}, bf16[3,90,1,34]{1,3,2,0:T(8,128)(2,1)S(1)}, u32[]{:S(2)}, u32[]{:S(2)}) collective-permute-start(bf16[3,90,1,34]{1,3,2,0:T(8,128)(2,1)S(1)} %get-tuple-element.15), channel_id=1, source_target_pairs={{4,0},{8,4},{12,8},{0,12},{5,1},{9,5},{13,9},{1,13},{6,2},{10,6},{... | collective-permute-start | bytes 55088 | tf_op jit(solution)/shard_map/ppermute | solution.py:27
  85.6 7.1 %collective-permute-start.20 = (bf16[2,90,2,16]{1,3,2,0:T(8,128)(2,1)S(1)}, bf16[2,90,2,16]{1,3,2,0:T(8,128)(2,1)S(1)}, u32[]{:S(2)}, u32[]{:S(2)}) collective-permute-start(bf16[2,90,2,16]{1,3,2,0:T(8,128)(2,1)S(1)} %pad_maximum_fusion.98), channel_id=1, source_target_pairs={{3,0},{0,1},{1,2},{2,3},{7,4},{4,5},{5,6},{6,7},{11,8},{8,9},{9,10... | collective-permute-start | bytes 34568 | tf_op jit(solution)/shard_map/ppermute | solution.py:16
  86.2 26.7 %collective-permute-start.21 = (bf16[2,90,4,2]{1,3,2,0:T(2,128)(2,1)S(1)}, bf16[2,90,4,2]{1,3,2,0:T(2,128)(2,1)S(1)}, u32[]{:S(2)}, u32[]{:S(2)}) collective-permute-start(bf16[2,90,4,2]{1,3,2,0:T(2,128)(2,1)S(1)} %get-tuple-element.53), channel_id=1, source_target_pairs={{3,0},{0,1},{1,2},{2,3},{7,4},{4,5},{5,6},{6,7},{11,8},{8,9},{9,10... | collective-permute-start | bytes 8648 | tf_op jit(solution)/shard_map/ppermute | solution.py:16
  87.6 24.5 %collective-permute-start.19 = (bf16[2,90,4,2]{1,3,2,0:T(2,128)(2,1)S(1)}, bf16[2,90,4,2]{1,3,2,0:T(2,128)(2,1)S(1)}, u32[]{:S(2)}, u32[]{:S(2)}) collective-permute-start(bf16[2,90,4,2]{1,3,2,0:T(2,128)(2,1)S(1)} %get-tuple-element.95), channel_id=1, source_target_pairs={{4,0},{8,4},{12,8},{0,12},{5,1},{9,5},{13,9},{1,13},{6,2},{10,6},{... | collective-permute-start | bytes 8648 | tf_op jit(solution)/shard_map/ppermute | solution.py:72
  92.8 19.3 %collective-permute-start.18 = (bf16[2,90,4,2]{1,3,2,0:T(2,128)(2,1)S(1)}, bf16[2,90,4,2]{1,3,2,0:T(2,128)(2,1)S(1)}, u32[]{:S(2)}, u32[]{:S(2)}) collective-permute-start(bf16[2,90,4,2]{1,3,2,0:T(2,128)(2,1)S(1)} %collective-permute-done.17), channel_id=1, source_target_pairs={{0,4},{4,8},{8,12},{12,0},{1,5},{5,9},{9,13},{13,1},{2,6},{6,10},{... | collective-permute-start | bytes 8648 | tf_op jit(solution)/shard_map/ppermute | solution.py:70
  112.9 5.8 %collective-permute-start.22 = (bf16[3,90,2,20]{1,3,2,0:T(8,128)(2,1)S(1)}, bf16[3,90,2,20]{1,3,2,0:T(8,128)(2,1)S(1)}, u32[]{:S(2)}, u32[]{:S(2)}) collective-permute-start(bf16[3,90,2,20]{1,3,2,0:T(8,128)(2,1)S(1)} %get-tuple-element.44), channel_id=1, source_target_pairs={{0,4},{4,8},{8,12},{12,0},{1,5},{5,9},{9,13},{13,1},{2,6},{6,10},{... | collective-permute-start | bytes 64808 | tf_op jit(solution)/shard_map/ppermute | solution.py:26
  113.0 5.7 %collective-permute-start.23 = (bf16[3,90,2,20]{1,3,2,0:T(8,128)(2,1)S(1)}, bf16[3,90,2,20]{1,3,2,0:T(8,128)(2,1)S(1)}, u32[]{:S(2)}, u32[]{:S(2)}) collective-permute-start(bf16[3,90,2,20]{1,3,2,0:T(8,128)(2,1)S(1)} %get-tuple-element.43), channel_id=1, source_target_pairs={{4,0},{8,4},{12,8},{0,12},{5,1},{9,5},{13,9},{1,13},{6,2},{10,6},{... | collective-permute-start | bytes 64808 | tf_op jit(solution)/shard_map/ppermute | solution.py:27
  120.8 7.0 %collective-permute-start.28 = (bf16[2,180,1,16]{1,3,2,0:T(8,128)(2,1)S(1)}, bf16[2,180,1,16]{1,3,2,0:T(8,128)(2,1)S(1)}, u32[]{:S(2)}, u32[]{:S(2)}) collective-permute-start(bf16[2,180,1,16]{1,3,2,0:T(8,128)(2,1)S(1)} %pad_maximum_fusion.100), channel_id=1, source_target_pairs={{3,0},{0,1},{1,2},{2,3},{7,4},{4,5},{5,6},{6,7},{11,8},{8,9},{9,10... | collective-permute-start | bytes 34568 | tf_op jit(solution)/shard_map/ppermute | solution.py:16
  121.3 26.6 %collective-permute-start.29 = (bf16[2,180,4,1]{1,3,2,0:T(2,128)(2,1)S(1)}, bf16[2,180,4,1]{1,3,2,0:T(2,128)(2,1)S(1)}, u32[]{:S(2)}, u32[]{:S(2)}) collective-permute-start(bf16[2,180,4,1]{1,3,2,0:T(2,128)(2,1)S(1)} %get-tuple-element.27), channel_id=1, source_target_pairs={{3,0},{0,1},{1,2},{2,3},{7,4},{4,5},{5,6},{6,7},{11,8},{8,9},{9,10... | collective-permute-start | bytes 8648 | tf_op jit(solution)/shard_map/ppermute | solution.py:16
  122.3 5.6 %collective-permute-start.25 = (bf16[2,180,4,1]{1,3,2,0:T(2,128)(2,1)S(1)}, bf16[2,180,4,1]{1,3,2,0:T(2,128)(2,1)S(1)}, u32[]{:S(2)}, u32[]{:S(2)}) collective-permute-start(bf16[2,180,4,1]{1,3,2,0:T(2,128)(2,1)S(1)} %get-tuple-element.73), channel_id=1, source_target_pairs={{0,4},{4,8},{8,12},{12,0},{1,5},{5,9},{9,13},{13,1},{2,6},{6,10},{... | collective-permute-start | bytes 8648 | tf_op jit(solution)/shard_map/ppermute | solution.py:70
  122.3 5.5 %collective-permute-start.27 = (bf16[2,180,4,1]{1,3,2,0:T(2,128)(2,1)S(1)}, bf16[2,180,4,1]{1,3,2,0:T(2,128)(2,1)S(1)}, u32[]{:S(2)}, u32[]{:S(2)}) collective-permute-start(bf16[2,180,4,1]{1,3,2,0:T(2,128)(2,1)S(1)} %get-tuple-element.73), channel_id=1, source_target_pairs={{4,0},{8,4},{12,8},{0,12},{5,1},{9,5},{13,9},{1,13},{6,2},{10,6},{... | collective-permute-start | bytes 8648 | tf_op jit(solution)/shard_map/ppermute | solution.py:72
  127.8 19.4 %collective-permute-start.26 = (bf16[2,180,4,1]{1,3,2,0:T(2,128)(2,1)S(1)}, bf16[2,180,4,1]{1,3,2,0:T(2,128)(2,1)S(1)}, u32[]{:S(2)}, u32[]{:S(2)}) collective-permute-start(bf16[2,180,4,1]{1,3,2,0:T(2,128)(2,1)S(1)} %collective-permute-done.25), channel_id=1, source_target_pairs={{0,4},{4,8},{8,12},{12,0},{1,5},{5,9},{9,13},{13,1},{2,6},{6,10},{... | collective-permute-start | bytes 8648 | tf_op jit(solution)/shard_map/ppermute | solution.py:70
  148.0 5.8 %collective-permute-start.30 = (bf16[3,180,1,18]{1,3,2,0:T(8,128)(2,1)S(1)}, bf16[3,180,1,18]{1,3,2,0:T(8,128)(2,1)S(1)}, u32[]{:S(2)}, u32[]{:S(2)}) collective-permute-start(bf16[3,180,1,18]{1,3,2,0:T(8,128)(2,1)S(1)} %get-tuple-element.26), channel_id=1, source_target_pairs={{0,4},{4,8},{8,12},{12,0},{1,5},{5,9},{9,13},{13,1},{2,6},{6,10},{... | collective-permute-start | bytes 58328 | tf_op jit(solution)/shard_map/ppermute | solution.py:26
  148.1 5.7 %collective-permute-start.31 = (bf16[3,180,1,18]{1,3,2,0:T(8,128)(2,1)S(1)}, bf16[3,180,1,18]{1,3,2,0:T(8,128)(2,1)S(1)}, u32[]{:S(2)}, u32[]{:S(2)}) collective-permute-start(bf16[3,180,1,18]{1,3,2,0:T(8,128)(2,1)S(1)} %get-tuple-element.25), channel_id=1, source_target_pairs={{4,0},{8,4},{12,8},{0,12},{5,1},{9,5},{13,9},{1,13},{6,2},{10,6},{... | collective-permute-start | bytes 58328 | tf_op jit(solution)/shard_map/ppermute | solution.py:27
  156.8 28.3 %collective-permute-start.37 = (bf16[2,270,8,1]{1,3,2,0:T(2,128)(2,1)S(1)}, bf16[2,270,8,1]{1,3,2,0:T(2,128)(2,1)S(1)}, u32[]{:S(2)}, u32[]{:S(2)}) collective-permute-start(bf16[2,270,8,1]{1,3,2,0:T(2,128)(2,1)S(1)} %pad_maximum_fusion.94), channel_id=1, source_target_pairs={{3,0},{0,1},{1,2},{2,3},{7,4},{4,5},{5,6},{6,7},{11,8},{8,9},{9,10... | collective-permute-start | bytes 25928 | tf_op jit(solution)/shard_map/ppermute | solution.py:16
  157.4 7.1 %collective-permute-start.36 = (bf16[2,270,1,32]{1,3,2,0:T(8,128)(2,1)S(1)}, bf16[2,270,1,32]{1,3,2,0:T(8,128)(2,1)S(1)}, u32[]{:S(2)}, u32[]{:S(2)}) collective-permute-start(bf16[2,270,1,32]{1,3,2,0:T(8,128)(2,1)S(1)} %fusion.160), channel_id=1, source_target_pairs={{3,0},{0,1},{1,2},{2,3},{7,4},{4,5},{5,6},{6,7},{11,8},{8,9},{9,10... | collective-permute-start | bytes 103688 | tf_op jit(solution)/shard_map/ppermute | solution.py:16
  158.5 5.9 %collective-permute-start.33 = (bf16[2,270,8,1]{1,3,2,0:T(2,128)(2,1)S(1)}, bf16[2,270,8,1]{1,3,2,0:T(2,128)(2,1)S(1)}, u32[]{:S(2)}, u32[]{:S(2)}) collective-permute-start(bf16[2,270,8,1]{1,3,2,0:T(2,128)(2,1)S(1)} %get-tuple-element.49), channel_id=1, source_target_pairs={{0,4},{4,8},{8,12},{12,0},{1,5},{5,9},{9,13},{13,1},{2,6},{6,10},{... | collective-permute-start | bytes 25928 | tf_op jit(solution)/shard_map/ppermute | solution.py:70
  158.6 5.9 %collective-permute-start.35 = (bf16[2,270,8,1]{1,3,2,0:T(2,128)(2,1)S(1)}, bf16[2,270,8,1]{1,3,2,0:T(2,128)(2,1)S(1)}, u32[]{:S(2)}, u32[]{:S(2)}) collective-permute-start(bf16[2,270,8,1]{1,3,2,0:T(2,128)(2,1)S(1)} %get-tuple-element.49), channel_id=1, source_target_pairs={{4,0},{8,4},{12,8},{0,12},{5,1},{9,5},{13,9},{1,13},{6,2},{10,6},{... | collective-permute-start | bytes 25928 | tf_op jit(solution)/shard_map/ppermute | solution.py:72
  164.5 20.1 %collective-permute-start.34 = (bf16[2,270,8,1]{1,3,2,0:T(2,128)(2,1)S(1)}, bf16[2,270,8,1]{1,3,2,0:T(2,128)(2,1)S(1)}, u32[]{:S(2)}, u32[]{:S(2)}) collective-permute-start(bf16[2,270,8,1]{1,3,2,0:T(2,128)(2,1)S(1)} %collective-permute-done.33), channel_id=1, source_target_pairs={{0,4},{4,8},{8,12},{12,0},{1,5},{5,9},{9,13},{13,1},{2,6},{6,10},{... | collective-permute-start | bytes 25928 | tf_op jit(solution)/shard_map/ppermute | solution.py:70
  185.4 6.4 %collective-permute-start.38 = (bf16[3,270,1,34]{1,3,2,0:T(8,128)(2,1)S(1)}, bf16[3,270,1,34]{1,3,2,0:T(8,128)(2,1)S(1)}, u32[]{:S(2)}, u32[]{:S(2)}) collective-permute-start(bf16[3,270,1,34]{1,3,2,0:T(8,128)(2,1)S(1)} %get-tuple-element.8), channel_id=1, source_target_pairs={{0,4},{4,8},{8,12},{12,0},{1,5},{5,9},{9,13},{13,1},{2,6},{6,10},{... | collective-permute-start | bytes 165248 | tf_op jit(solution)/shard_map/ppermute | solution.py:26
  185.4 6.4 %collective-permute-start.39 = (bf16[3,270,1,34]{1,3,2,0:T(8,128)(2,1)S(1)}, bf16[3,270,1,34]{1,3,2,0:T(8,128)(2,1)S(1)}, u32[]{:S(2)}, u32[]{:S(2)}) collective-permute-start(bf16[3,270,1,34]{1,3,2,0:T(8,128)(2,1)S(1)} %get-tuple-element.7), channel_id=1, source_target_pairs={{4,0},{8,4},{12,8},{0,12},{5,1},{9,5},{13,9},{1,13},{6,2},{10,6},{... | collective-permute-start | bytes 165248 | tf_op jit(solution)/shard_map/ppermute | solution.py:27
  (18 other events, 150.7 us)
Sparse Core Ops, SparseCore 0:
  56.0 20.0 reduce-scatter.6
